TPU v7x, 32 devices: a whole 2x2x4 slice. The times are simulated.
32 devices in a mesh: dp: 2 (over core), ctx: 16 (over z, y, x).
Axes of the slice: x: 2, y: 2, z: 4, core: 2. Of those that a mesh axis runs over, the one named last changes fastest.
Arguments:
- doc_lengths: int32 [8], P('dp'), parts along dimension 0, may hold values from 1 to 1024, 2048 in all
- assignment: int32 [128], P('dp'), parts along dimension 0, may hold values from 0 to 63, each once
- queries: bfloat16 [4096, 4096], P(('dp', 'ctx')), parts along dimension 0, may hold values from -6 to 6
- key_state_rows: bfloat16 [4096, 512], P(('dp', 'ctx')), parts along dimension 0, may hold values from -6 to 6
- value_state_rows: bfloat16 [4096, 512], P(('dp', 'ctx')), parts along dimension 0, may hold values from -6 to 6
- out_grad: bfloat16 [4096, 4096], P(('dp', 'ctx')), parts along dimension 0, may hold values from -6 to 6
Outputs:
- attention_out: bfloat16 [4096, 4096], P(('dp', 'ctx')), parts along dimension 0
- query_grad: bfloat16 [4096, 4096], P(('dp', 'ctx')), parts along dimension 0
- key_gradient: bfloat16 [4096, 512], P(('dp', 'ctx')), parts along dimension 0
- value_gradient: bfloat16 [4096, 512], P(('dp', 'ctx')), parts along dimension 0
There are 2 independent parts, one for each index of `dp`. A program takes and returns all parts, laid end to end along the dimension named above; each array names one. Nothing has to cross between parts.
Inputs may be any that keep to these rules, and one draw needn't show every extreme that they name: `assignment`: each of 0 to 63 once.
All inputs are finite; a program needn't handle non-finite values.
Results may differ from a plain program's by a relative error of at most 0.015.
Values may be sent and summed in bfloat16 or wider, within the bound.
A program may use at most 128 MiB of HBM per device.

v0:
```python
import jax
import jax.numpy as jnp
from jax import lax
from jax.sharding import PartitionSpec as P

BLK = 32
MOST = 1024
HEAD_SIZE = 128


def body(doc_lengths, assignment, queries, key_state_rows, value_state_rows, out_grad):
    row_count = queries.shape[0]
    head_width = key_state_rows.shape[1]
    kv_heads = head_width // HEAD_SIZE
    group_width = queries.shape[1] // head_width
    block_count = row_count // BLK
    span_rows = MOST + BLK
    blocks_all = assignment.shape[0]
    score_scale = HEAD_SIZE ** (-0.5)
    doc_bounds = jnp.cumsum(doc_lengths)
    slot_of = (
        jnp.zeros((blocks_all,), jnp.int32)
        .at[assignment]
        .set(jnp.arange(blocks_all, dtype=jnp.int32))
    )
    own_blocks = lax.dynamic_slice_in_dim(
        assignment, lax.axis_index("ctx") * block_count, block_count
    )
    query_blocks = queries.reshape(block_count, BLK, kv_heads, group_width, HEAD_SIZE)
    grad_blocks = out_grad.reshape(block_count, BLK, kv_heads, group_width, HEAD_SIZE)

    def layout(seq_block):
        block_end = (seq_block + 1) * BLK
        key_place = block_end - span_rows + jnp.arange(span_rows, dtype=jnp.int32)
        query_place = seq_block * BLK + jnp.arange(BLK, dtype=jnp.int32)
        key_doc = jnp.sum((doc_bounds[None, :] <= key_place[:, None]).astype(jnp.int32), axis=1)
        query_doc = jnp.sum((doc_bounds[None, :] <= query_place[:, None]).astype(jnp.int32), axis=1)
        allowed = (
            (key_place[None, :] >= 0)
            & (key_doc[None, :] == query_doc[:, None])
            & (key_place[None, :] <= query_place[:, None])
        )
        return (block_end, allowed)

    def windows(padded_pair, block_end):
        window_keys = lax.dynamic_slice_in_dim(padded_pair[0], block_end, span_rows, 0).reshape(
            span_rows, kv_heads, HEAD_SIZE
        )
        window_values = lax.dynamic_slice_in_dim(padded_pair[1], block_end, span_rows, 0).reshape(
            span_rows, kv_heads, HEAD_SIZE
        )
        return (window_keys, window_values)

    gathered = (
        lax.all_gather(key_state_rows, "ctx", axis=0, tiled=True),
        lax.all_gather(value_state_rows, "ctx", axis=0, tiled=True),
    )
    padding = jnp.zeros((span_rows, head_width), jnp.bfloat16)
    ordered = []
    for gathered_rows in gathered:
        blocked = gathered_rows.reshape(blocks_all, BLK, head_width)[slot_of]
        ordered.append(
            jnp.concatenate([padding, blocked.reshape(blocks_all * BLK, head_width)], axis=0)
        )
    padded_pair = (ordered[0], ordered[1])

    def forward_block(slices):
        block_query, seq_block = slices
        block_end, allowed = layout(seq_block)
        window_keys, window_values = windows(padded_pair, block_end)
        scores = (
            jnp.einsum(
                "qgjd,kgd->gjqk", block_query, window_keys, preferred_element_type=jnp.float32
            )
            * score_scale
        )
        masked = jnp.where(allowed, scores, -jnp.inf)
        row_top = jnp.max(masked, axis=-1, keepdims=True)
        log_total = row_top + jnp.log(jnp.sum(jnp.exp(masked - row_top), axis=-1, keepdims=True))
        attention = jnp.where(allowed, jnp.exp(scores - log_total), 0.0).astype(jnp.bfloat16)
        output = jnp.einsum(
            "gjqk,kgd->qgjd", attention, window_values, preferred_element_type=jnp.float32
        )
        return (output.astype(jnp.bfloat16), log_total)

    out_blocks, total_blocks = lax.map(forward_block, (query_blocks, own_blocks))

    def backward_step(buffers, slices):
        block_query, block_grad, block_out, log_total, seq_block = slices
        block_end, allowed = layout(seq_block)
        window_keys, window_values = windows(padded_pair, block_end)
        scores = (
            jnp.einsum(
                "qgjd,kgd->gjqk", block_query, window_keys, preferred_element_type=jnp.float32
            )
            * score_scale
        )
        attention = jnp.where(allowed, jnp.exp(scores - log_total), 0.0)
        attention_b = attention.astype(jnp.bfloat16)
        row_delta = jnp.sum(block_grad.astype(jnp.float32) * block_out.astype(jnp.float32), axis=-1)
        row_delta = jnp.transpose(row_delta, (1, 2, 0))[..., None]
        grad_weights = jnp.einsum(
            "qgjd,kgd->gjqk", block_grad, window_values, preferred_element_type=jnp.float32
        )
        dscore = (attention * (grad_weights - row_delta) * score_scale).astype(jnp.bfloat16)
        query_term = jnp.einsum(
            "gjqk,kgd->qgjd", dscore, window_keys, preferred_element_type=jnp.float32
        ).astype(jnp.bfloat16)
        key_term = jnp.einsum(
            "gjqk,qgjd->kgd", dscore, block_query, preferred_element_type=jnp.float32
        )
        value_term = jnp.einsum(
            "gjqk,qgjd->kgd", attention_b, block_grad, preferred_element_type=jnp.float32
        )
        key_sum, value_sum = buffers
        key_sum = lax.dynamic_update_slice_in_dim(
            key_sum,
            lax.dynamic_slice_in_dim(key_sum, block_end, span_rows, 0) + key_term,
            block_end,
            0,
        )
        value_sum = lax.dynamic_update_slice_in_dim(
            value_sum,
            lax.dynamic_slice_in_dim(value_sum, block_end, span_rows, 0) + value_term,
            block_end,
            0,
        )
        return ((key_sum, value_sum), query_term)

    empty_sums = (
        jnp.zeros((blocks_all * BLK + span_rows, kv_heads, HEAD_SIZE), jnp.float32),
        jnp.zeros((blocks_all * BLK + span_rows, kv_heads, HEAD_SIZE), jnp.float32),
    )
    sums, query_terms = lax.scan(
        backward_step, empty_sums, (query_blocks, grad_blocks, out_blocks, total_blocks, own_blocks)
    )

    def to_slots(buffer):
        trimmed = buffer[span_rows:].reshape(blocks_all, BLK, head_width)
        return trimmed[assignment].reshape(blocks_all * BLK, head_width)

    key_slots = to_slots(sums[0])
    value_slots = to_slots(sums[1])
    both_slots = jnp.concatenate([key_slots, value_slots], axis=1)
    reduced = lax.psum_scatter(
        both_slots.astype(jnp.bfloat16), "ctx", scatter_dimension=0, tiled=True
    ).astype(jnp.float32)
    key_gradient = reduced[:, :head_width]
    value_gradient = reduced[:, head_width:]
    attention_out = out_blocks.reshape(row_count, -1)
    query_grad = query_terms.reshape(row_count, -1)
    return (
        attention_out,
        query_grad,
        key_gradient.astype(jnp.bfloat16),
        value_gradient.astype(jnp.bfloat16),
    )


def solution(mesh):
    return jax.shard_map(
        body,
        mesh=mesh,
        in_specs=(
            P("dp"),
            P("dp"),
            P(("dp", "ctx"), None),
            P(("dp", "ctx"), None),
            P(("dp", "ctx"), None),
            P(("dp", "ctx"), None),
        ),
        out_specs=(
            P(("dp", "ctx"), None),
            P(("dp", "ctx"), None),
            P(("dp", "ctx"), None),
            P(("dp", "ctx"), None),
        ),
        check_vma=False,
    )
```

profile of v0, /device:TPU:0, one launch (start us, length us, event | category | flops | bytes accessed | tf_op | source)
XLA Modules:
  0.0 441.7 jit_solution(7250154697642595946)
XLA Ops:
  14.0 60.2 %all-gather.3.cloned.1.call-done = bf16[2048,512]{1,0:T(8,128)(2,1)} async-done(((bf16[128,512]{1,0:T(8,128)(2,1)}), bf16[2048,512]{1,0:T(8,128)(2,1)}) %all-gather.3.cloned.1.call-update) | async-done | bytes 2097168 | tf_op jit(solution)/shard_map/all_gather | solution.py:56
  74.2 2.3 gather_fusion
  76.5 59.9 %all-gather.5.cloned.1.call-done = bf16[2048,512]{1,0:T(8,128)(2,1)} async-done(((bf16[128,512]{1,0:T(8,128)(2,1)}), bf16[2048,512]{1,0:T(8,128)(2,1)}) %all-gather.5.cloned.1.call-update) | async-done | bytes 2097168 | tf_op jit(solution)/shard_map/all_gather | solution.py:55
  136.4 3.6 gather_fusion.1
  140.0 1.9 concatenate.10
  142.6 1.9 concatenate.11
  144.5 49.9 %while.30 = (s32[]{:T(128)}, bf16[4,32,4,8,128]{4,1,3,2,0:T(8,128)(2,1)}, f32[4,4,8,32,1]{3,2,1,4,0:T(8,128)S(1)}, s32[4]{0:T(128)S(1)}, bf16[3104,512]{1,0:T(8,...) while((s32[]{:T(128)}, ...), condition=%wide.region_7.8_spmd, body=%wide.region_2.7_spmd.sunk | while | flops 563660608 | bytes 42250868 | solution.py:86
  146.5 1.7 constant_dynamic-slice_fusion.8
  148.5 1.9 fusion.70
  152.9 4.0 fusion.71
  159.0 1.7 constant_dynamic-slice_fusion.8
  161.0 1.9 fusion.70
  165.4 4.0 fusion.71
  173.5 1.9 fusion.70
  177.9 4.0 fusion.71
  184.0 1.7 constant_dynamic-slice_fusion.8
  186.0 1.9 fusion.70
  190.4 4.0 fusion.71
  194.4 3.1 broadcast.121
  197.5 3.1 broadcast.121.clone
  200.6 95.6 %while.31 = (s32[]{:T(128)}, f32[3104,4,128]{2,0,1:T(8,128)}, f32[3104,4,128]{2,0,1:T(8,128)}, bf16[4,32,4,8,128]{4,3,2,1,0:T(8,128)(2,1)}, s32[4]{0:T(128)S(1)}...) while((s32[]{:T(128)}, f32[3104,4,128]{2,0,1:T(8,128)}, ...), condition=%wide.region_12.13_spmd, body=%wide.region_8.12_spmd.sunk | while | flops 1394657024 | bytes 57162932 | solution.py:134
  204.8 4.3 fusion.80
  211.5 3.2 fusion.82
  214.8 4.2 fusion.83
  220.5 3.9 fusion.84
  228.7 4.3 fusion.80
  235.4 3.2 fusion.82
  238.6 4.2 fusion.83
  244.4 3.9 fusion.84
  250.6 1.7 constant_dynamic-slice_fusion.9
  252.6 4.3 fusion.80
  259.3 3.2 fusion.82
  262.5 4.2 fusion.83
  268.3 4.0 fusion.84
  276.5 4.3 fusion.80
  283.2 3.2 fusion.82
  286.4 4.2 fusion.83
  292.2 4.0 fusion.84
  296.2 2.5 slice.14
  298.7 11.0 %copy.34 = bf16[2048,4,128]{2,1,0:T(4,128)(2,1)} copy(bf16[2048,4,128]{2,0,1:T(8,128)(2,1)S(1)} %slice.14) | data formatting | bytes 4194304 | tf_op jit(solution)/shard_map/slice | solution.py:139
  309.6 2.7 reshape.193
  312.4 2.5 slice.15
  314.9 10.7 %copy.35 = bf16[2048,4,128]{2,1,0:T(4,128)(2,1)} copy(bf16[2048,4,128]{2,0,1:T(8,128)(2,1)S(1)} %slice.15) | data formatting | bytes 4194304 | tf_op jit(solution)/shard_map/slice | solution.py:139
  325.6 4.1 reshape.195
  329.7 2.0 gather_fusion.2
  331.7 3.7 gather_fusion.3
  335.4 4.1 pad_maximum_fusion
  343.7 89.8 %reduce-scatter.2.cloned.1.call-done = bf16[128,1024]{1,0:T(8,128)(2,1)} async-done(((bf16[2048,1024]{1,0:T(8,128)(2,1)}), bf16[128,1024]{1,0:T(8,128)(2,1)}) %reduce-scatter.2.cloned.1.call-update) | async-done | bytes 262160 | tf_op jit(solution)/shard_map/reduce_scatter | solution.py:145
  (170 shorter events, 55.2 us)
Async XLA Ops:
  7.2 4.4 %copy-start.6 = (s32[4]{0:T(128)S(1)}, s32[4]{0:T(128)}, u32[]{:S(2)}) copy-start(s32[4]{0:T(128)} %param.10) | copy-start | bytes 52
  7.2 4.6 %copy-start.4 = (bf16[128,4096]{1,0:T(8,128)(2,1)S(1)}, bf16[128,4096]{1,0:T(8,128)(2,1)}, u32[]{:S(2)}) copy-start(bf16[128,4096]{1,0:T(8,128)(2,1)} %param.15) | copy-start | bytes 3145732
  7.2 67.0 %all-gather.3.cloned.1.call-start = ((), (), s32[]{:S(2)}) async-start(), calls=%async_computation.1 | async-start | bytes 2228224 | tf_op jit(solution)/shard_map/all_gather | solution.py:56
  7.9 128.5 %all-gather.5.cloned.1.call-start = ((), (), s32[]{:S(2)}) async-start(), calls=%async_computation.2 | async-start | bytes 2228224 | tf_op jit(solution)/shard_map/all_gather | solution.py:55
  8.7 424.8 %reduce-scatter.2.cloned.1.call-start = ((), (), s32[]{:S(2)}) async-start(), calls=%async_computation.3 | async-start | bytes 4456448 | tf_op jit(solution)/shard_map/reduce_scatter | solution.py:145
  10.2 2.9 copy-start.7
  140.0 2.6 copy-start.1
  150.5 2.1 copy-start
  163.0 2.1 copy-start
  175.4 2.1 copy-start
  187.9 2.1 copy-start
  214.7 5.8 %slice-start = ((s8[4718592]{0:T(1024)(128)(4,1)}), s8[4194304]{0:T(1024)(128)(4,1)S(1)}, s32[]{:S(2)}) async-start(s8[4718592]{0:T(1024)(128)(4,1)} %bitcast.173), calls=%async_computation.4 | async-start | bytes 8388608 | tf_op jit(solution)/shard_map/while
  214.7 5.8 %slice-start.1 = ((s8[4718592]{0:T(1024)(128)(4,1)}), s8[524288]{0:T(1024)(128)(4,1)S(1)}, s32[]{:S(2)}) async-start(s8[4718592]{0:T(1024)(128)(4,1)} %bitcast.173), calls=%async_computation.5 | async-start | bytes 1048576 | tf_op jit(solution)/shard_map/while
  238.6 5.8 %slice-start = ((s8[4718592]{0:T(1024)(128)(4,1)}), s8[4194304]{0:T(1024)(128)(4,1)S(1)}, s32[]{:S(2)}) async-start(s8[4718592]{0:T(1024)(128)(4,1)} %bitcast.173), calls=%async_computation.4 | async-start | bytes 8388608 | tf_op jit(solution)/shard_map/while
  238.6 5.8 %slice-start.1 = ((s8[4718592]{0:T(1024)(128)(4,1)}), s8[524288]{0:T(1024)(128)(4,1)S(1)}, s32[]{:S(2)}) async-start(s8[4718592]{0:T(1024)(128)(4,1)} %bitcast.173), calls=%async_computation.5 | async-start | bytes 1048576 | tf_op jit(solution)/shard_map/while
  262.5 5.8 %slice-start = ((s8[4718592]{0:T(1024)(128)(4,1)}), s8[4194304]{0:T(1024)(128)(4,1)S(1)}, s32[]{:S(2)}) async-start(s8[4718592]{0:T(1024)(128)(4,1)} %bitcast.173), calls=%async_computation.4 | async-start | bytes 8388608 | tf_op jit(solution)/shard_map/while
  262.5 5.8 %slice-start.1 = ((s8[4718592]{0:T(1024)(128)(4,1)}), s8[524288]{0:T(1024)(128)(4,1)S(1)}, s32[]{:S(2)}) async-start(s8[4718592]{0:T(1024)(128)(4,1)} %bitcast.173), calls=%async_computation.5 | async-start | bytes 1048576 | tf_op jit(solution)/shard_map/while
  286.4 5.8 %slice-start = ((s8[4718592]{0:T(1024)(128)(4,1)}), s8[4194304]{0:T(1024)(128)(4,1)S(1)}, s32[]{:S(2)}) async-start(s8[4718592]{0:T(1024)(128)(4,1)} %bitcast.173), calls=%async_computation.4 | async-start | bytes 8388608 | tf_op jit(solution)/shard_map/while
  286.4 5.8 %slice-start.1 = ((s8[4718592]{0:T(1024)(128)(4,1)}), s8[524288]{0:T(1024)(128)(4,1)S(1)}, s32[]{:S(2)}) async-start(s8[4718592]{0:T(1024)(128)(4,1)} %bitcast.173), calls=%async_computation.5 | async-start | bytes 1048576 | tf_op jit(solution)/shard_map/while
  331.7 3.8 copy-start.2
  339.5 1.2 copy-start.3
  339.5 1.6 copy-start.5
Sparse Core Ops, SparseCore 0:
  10.8 63.3 all-gather.2
  77.0 59.3 all-gather.4
  339.7 93.7 reduce-scatter.1
where the time goes:
time: 444 us; the launch traced here: 442 us
  waiting for transfers between devices  211 us (48%)
  local copies, waits for them, and re-layouts  101 us (23%)
  matrix products  89.4 us (20%)
  other arithmetic  15.7 us (4%)
  between operations  13.9 us (3%)
  loops' own time  10.4 us (2%)
    reduce_scatter x1, waiting for transfers between devices, body(): lax.psum_scatter(both_slots.astype(jnp.bfloat16), 'ctx', scatter_dimensio...  89.8 us
    all_gather x1, waiting for transfers between devices, body(): lax.all_gather(value_state_rows, 'ctx', axis=0, tiled=True)  60.2 us
    all_gather x1, waiting for transfers between devices, body(): lax.all_gather(key_state_rows, 'ctx', axis=0, tiled=True)  59.9 us
    slice x4, local copies, waits for them, and re-layouts, to_slots(): trimmed = buffer[span_rows:].reshape(blocks_all, BLK, head_width)  26.6 us
    dot_general x4, matrix products, backward_step(): jnp.einsum('qgjd,kgd->gjqk', block_query, window_keys, preferred_element_...  17.1 us
    dot_general x4, matrix products, backward_step(): jnp.einsum('gjqk,qgjd->kgd', dscore, block_query, preferred_element_type=...  16.7 us
    dot_general x4, matrix products, forward_block(): jnp.einsum('gjqk,kgd->qgjd', attention, window_values, preferred_element_...  16.2 us
    dot_general x4, matrix products, backward_step(): jnp.einsum('gjqk,qgjd->kgd', attention_b, block_grad, preferred_element_t...  15.8 us
  transfers between devices with their start and end apart: 3, of which 3 were waited for; matrix products, arithmetic and copies ran while one was open for 2% of the time, Pallas kernels for 0%

commit v1 on v0

v1 whole, which is shorter than its diff:
```python
import functools

import jax
import jax.numpy as jnp
from jax import lax
from jax.experimental import pallas as pl
from jax.experimental.pallas import tpu as pltpu
from jax.sharding import PartitionSpec as P

BLK = 32
HEAD = 128
LOG2E = 1.4426950408889634
F32 = jnp.float32
BF16 = jnp.bfloat16


def nt(a, b):
    return lax.dot_general(a, b, (((1,), (1,)), ((), ())), preferred_element_type=F32)


def nn(a, b):
    return jnp.dot(a, b, preferred_element_type=F32)


def kernel(
    planes, groups, pairs,
    bias_ref, q_ref, k_ref, v_ref, do_ref,
    out_ref, dq_ref, dk_ref, dv_ref,
    kvb, part, half, zbuf, lastb, s_buf, e_buf, kt, vt, acc,
    ag_send, ag_recv, rs_send, rs_recv,
):
    rows = q_ref.shape[0]
    tile = 4 * rows
    scale = HEAD ** (-0.5)
    me = lax.axis_index("ctx")
    x = lax.rem(me, 2)
    y = lax.rem(me // 2, 2)
    z = me // 4
    peer_x = me + 1 - 2 * x
    peer_y = me + 2 - 4 * y
    top = planes - 1

    def remote(src, dst, send, recv, device):
        return pltpu.make_async_remote_copy(
            src_ref=src, dst_ref=dst, send_sem=send, recv_sem=recv,
            device_id={"ctx": device}, device_id_type=pl.DeviceIdType.MESH,
        )

    def ag_copy(g, v, index, ref, device):
        return remote(ref, ref, ag_send.at[g, v, index], ag_recv.at[g, v, index], device)

    def pair_of(g, v, plane):
        return kvb.at[g, 0, plane, y] if v == 0 else kvb.at[g, 1, plane, :, x]

    def ag_first(g, v):
        return ag_copy(g, v, 0, kvb.at[g, v, z, y, x], peer_x if v == 0 else peer_y)

    def ag_first_in(g, v):
        ref = kvb.at[g, 0, z, y, 1 - x] if v == 0 else kvb.at[g, 1, z, 1 - y, x]
        return ag_copy(g, v, 0, ref, peer_x if v == 0 else peer_y)

    def ag_up(g, v, j, plane):
        return ag_copy(g, v, 1 + j, pair_of(g, v, plane), me + 4)

    def ag_down(g, v, j, plane):
        return ag_copy(g, v, planes + j, pair_of(g, v, plane), me - 4)

    def ag_last(g, v, plane):
        return ag_copy(g, v, 2 * planes - 1 + plane, pair_of(g, v, plane), peer_y if v == 0 else peer_x)

    def ag_last_in(g, v, plane):
        ref = kvb.at[g, 0, plane, 1 - y] if v == 0 else kvb.at[g, 1, plane, :, 1 - x]
        return ag_copy(g, v, 2 * planes - 1 + plane, ref, peer_y if v == 0 else peer_x)

    def ag_step(k, g):
        for v in range(2):
            if k == 0:
                ag_first(g, v).start()
            elif k == 1:
                ag_first_in(g, v).wait_recv()

                @pl.when(z < top)
                def _():
                    ag_up(g, v, 0, z).start()

                @pl.when(z > 0)
                def _():
                    ag_down(g, v, 0, z).start()

                ag_last(g, v, z).start()
            elif k <= planes:
                j = k - 1

                @pl.when(z >= j)
                def _():
                    ag_up(g, v, j - 1, z - j).wait_recv()
                    if j < top:
                        @pl.when(z < top)
                        def _():
                            ag_up(g, v, j, z - j).start()
                    ag_last(g, v, z - j).start()

                @pl.when(z + j <= top)
                def _():
                    ag_down(g, v, j - 1, z + j).wait_recv()
                    if j < top:
                        @pl.when(z > 0)
                        def _():
                            ag_down(g, v, j, z + j).start()
                    ag_last(g, v, z + j).start()
            else:
                for plane in range(planes):
                    ag_last_in(g, v, plane).wait_recv()
                    ag_last(g, v, plane).wait_send()
                ag_first(g, v).wait_send()
                for j in range(top):
                    @pl.when(jnp.logical_and(z < top, z >= j))
                    def _():
                        ag_up(g, v, j, z - j).wait_send()

                    @pl.when(jnp.logical_and(z > 0, z + j <= top))
                    def _():
                        ag_down(g, v, j, z + j).wait_send()

    def rs_half(g, v):
        src = part.at[g, 0, :, 1 - y] if v == 0 else part.at[g, 1, :, :, 1 - x]
        return remote(src, half.at[g, v], rs_send.at[g, v, 0], rs_recv.at[g, v, 0],
                      peer_y if v == 0 else peer_x)

    def rs_flow(g, v, way, t):
        index = 1 + way * planes + t
        return remote(half.at[g, v, t], zbuf.at[g, v, way, t], rs_send.at[g, v, index],
                      rs_recv.at[g, v, index], me + 4 - 8 * way)

    def rs_last(g, v):
        index = 1 + 2 * planes
        src = half.at[g, 0, z, 1 - x] if v == 0 else half.at[g, 1, z, 1 - y]
        return remote(src, lastb.at[g, v], rs_send.at[g, v, index], rs_recv.at[g, v, index],
                      peer_x if v == 0 else peer_y)

    def rs_step(k, g):
        for v in range(2):
            if k == 0:
                rs_half(g, v).start()
                continue
            if k == 1:
                rs_half(g, v).wait_recv()
                own = part[g, 0, :, y] if v == 0 else part[g, 1, :, :, x]
                half[g, v] = (half[g, v].astype(F32) + own.astype(F32)).astype(BF16)
            if k <= planes:
                s = k - 1
                for way in range(2):
                    place = z if way == 0 else top - z
                    dist = top - (s - place)
                    t = dist if way == 0 else top - dist

                    @pl.when(jnp.logical_and(s >= place, dist >= place))
                    def _():
                        @pl.when(place > 0)
                        def _():
                            rs_flow(g, v, way, t).wait_recv()
                            half[g, v, t] = (
                                half[g, v, t].astype(F32) + zbuf[g, v, way, t].astype(F32)
                            ).astype(BF16)

                        @pl.when(dist > place)
                        def _():
                            rs_flow(g, v, way, t).start()
            if k == planes:
                rs_last(g, v).start()
            if k == planes + 1:
                rs_last(g, v).wait_recv()
                own = half[g, 0, z, x] if v == 0 else half[g, 1, z, y]
                total = (own.astype(F32) + lastb[g, v].astype(F32)).astype(BF16)
                cols = pl.ds(pl.multiple_of(g * HEAD, HEAD), HEAD)
                (dk_ref if v == 0 else dv_ref)[:, cols] = total
                rs_half(g, v).wait_send()
                rs_last(g, v).wait_send()
                for t in range(planes):
                    @pl.when(t > z)
                    def _():
                        rs_flow(g, v, 0, t).wait_send()

                    @pl.when(t < z)
                    def _():
                        rs_flow(g, v, 1, t).wait_send()

    steps = planes + 2

    barrier = pltpu.get_barrier_semaphore()
    for peer in (peer_x, peer_y):
        pl.semaphore_signal(barrier, inc=1, device_id={"ctx": peer}, device_id_type=pl.DeviceIdType.MESH)

    @pl.when(z < top)
    def _():
        pl.semaphore_signal(barrier, inc=1, device_id={"ctx": me + 4}, device_id_type=pl.DeviceIdType.MESH)

    @pl.when(z > 0)
    def _():
        pl.semaphore_signal(barrier, inc=1, device_id={"ctx": me - 4}, device_id_type=pl.DeviceIdType.MESH)

    for g in range(groups):
        kvb[g, 0, z, y, x] = k_ref[:, g * HEAD:(g + 1) * HEAD]
        kvb[g, 1, z, y, x] = v_ref[:, g * HEAD:(g + 1) * HEAD]
    pl.semaphore_wait(barrier, 2 + (z < top).astype(jnp.int32) + (z > 0).astype(jnp.int32))

    for g in range(groups):
        ag_step(0, g)
    for k in range(1, steps):
        ag_step(k, 0)

    points = 2 * pairs

    def beside(place, g, p):
        for k in range(steps):
            point = min(k, points - 1)
            if point % 2 != place:
                continue

            @pl.when(p == point // 2)
            def _():
                if k > 0:
                    @pl.when(g < groups - 1)
                    def _():
                        ag_step(k, g + 1)

                @pl.when(g > 0)
                def _():
                    rs_step(k, g - 1)

    def keys(g, v, t):
        return kvb[g, v, t].reshape(tile, HEAD)

    def head(g, carry):
        for t in range(planes):
            kt[:, t * tile:(t + 1) * tile] = keys(g, 0, t).T
            vt[:, t * tile:(t + 1) * tile] = keys(g, 1, t).T
        acc[...] = jnp.zeros_like(acc)

        def pair(p, carry):
            start = pl.multiple_of((g * pairs + p) * 2 * HEAD, HEAD)
            col0 = pl.ds(start, HEAD)
            col1 = pl.ds(pl.multiple_of(start + HEAD, HEAD), HEAD)
            q2 = jnp.concatenate([q_ref[:, col0], q_ref[:, col1]], axis=0)
            wide = q2.shape[0]
            most = jnp.full((8, wide), -jnp.inf, F32)
            for t in range(planes):
                b = bias_ref[t * tile:(t + 1) * tile, :]
                s = nt(keys(g, 0, t), q2) + jnp.concatenate([b, b], axis=1)
                s_buf[t * tile:(t + 1) * tile, :] = s
                most = jnp.maximum(most, jnp.max(s.reshape(tile // 8, 8, wide), axis=0))
            beside(0, g, p)
            lift = jnp.max(most, axis=0, keepdims=True) * (scale * LOG2E)
            total = jnp.zeros((8, wide), F32)
            o_t = jnp.zeros((HEAD, wide), F32)
            for t in range(planes):
                e = jnp.exp2(s_buf[t * tile:(t + 1) * tile, :] * (scale * LOG2E) - lift)
                total = total + jnp.sum(e.reshape(tile // 8, 8, wide), axis=0)
                eb = e.astype(BF16)
                e_buf[t * tile:(t + 1) * tile, :] = eb
                o_t = o_t + nn(vt[:, t * tile:(t + 1) * tile], eb)
            inv = 1.0 / jnp.sum(total, axis=0, keepdims=True)
            o_t = (o_t * inv).astype(BF16).astype(F32)
            o2 = o_t.T.astype(BF16)
            out_ref[:, col0] = o2[:rows]
            out_ref[:, col1] = o2[rows:]
            do2 = jnp.concatenate([do_ref[:, col0], do_ref[:, col1]], axis=0).astype(F32)
            delta = jnp.sum(do2.T * o_t, axis=0, keepdims=True) * inv
            dos = (do2 * jnp.broadcast_to(inv, (HEAD, wide)).T).astype(BF16)
            dq_t = jnp.zeros((HEAD, wide), F32)
            for t in range(planes):
                span = slice(t * tile, (t + 1) * tile)
                dp = nt(keys(g, 1, t), dos)
                eb = e_buf[span, :]
                ds = (eb.astype(F32) * (dp - delta)).astype(BF16)
                acc[0, span, :] += nn(ds, q2)
                acc[1, span, :] += nn(eb, dos)
                dq_t = dq_t + nn(kt[:, span], ds)
            dq2 = (dq_t * scale).T.astype(BF16)
            dq_ref[:, col0] = dq2[:rows]
            dq_ref[:, col1] = dq2[rows:]
            beside(1, g, p)
            return carry

        lax.fori_loop(0, pairs, pair, 0)
        for t in range(planes):
            span = slice(t * tile, (t + 1) * tile)
            part[g, 0, t] = (acc[0, span, :] * scale).astype(BF16).reshape(2, 2, rows, HEAD)
            part[g, 1, t] = acc[1, span, :].astype(BF16).reshape(2, 2, rows, HEAD)
        return carry

    lax.fori_loop(0, groups, head, 0)
    for k in range(steps):
        rs_step(k, groups - 1)


def body(doc_lengths, assignment, queries, key_state_rows, value_state_rows, out_grad):
    rows = queries.shape[0]
    blocks = assignment.shape[0]
    total = blocks * BLK
    devices = total // rows
    planes = devices // 4
    groups = key_state_rows.shape[1] // HEAD
    pairs = queries.shape[1] // key_state_rows.shape[1] // 2
    bounds = jnp.cumsum(doc_lengths)
    per = rows // BLK
    own = lax.dynamic_slice_in_dim(assignment, lax.axis_index("ctx") * per, per)
    offset = jnp.arange(BLK, dtype=jnp.int32)
    key_place = (assignment[:, None] * BLK + offset[None, :]).reshape(-1)
    query_place = (own[:, None] * BLK + offset[None, :]).reshape(-1)
    key_doc = jnp.sum((bounds[None, :] <= key_place[:, None]).astype(jnp.int32), axis=1)
    query_doc = jnp.sum((bounds[None, :] <= query_place[:, None]).astype(jnp.int32), axis=1)
    allowed = (key_doc[:, None] == query_doc[None, :]) & (key_place[:, None] <= query_place[None, :])
    bias = jnp.where(allowed, 0.0, -1e30).astype(F32)

    ag_sems = 3 * planes - 1
    rs_sems = 2 * planes + 2
    vmem = pl.BlockSpec(memory_space=pltpu.VMEM)
    return pl.pallas_call(
        functools.partial(kernel, planes, groups, pairs),
        out_shape=(
            jax.ShapeDtypeStruct(queries.shape, BF16),
            jax.ShapeDtypeStruct(queries.shape, BF16),
            jax.ShapeDtypeStruct(key_state_rows.shape, BF16),
            jax.ShapeDtypeStruct(key_state_rows.shape, BF16),
        ),
        in_specs=[vmem] * 5,
        out_specs=(vmem,) * 4,
        scratch_shapes=[
            pltpu.VMEM((groups, 2, planes, 2, 2, rows, HEAD), BF16),
            pltpu.VMEM((groups, 2, planes, 2, 2, rows, HEAD), BF16),
            pltpu.VMEM((groups, 2, planes, 2, rows, HEAD), BF16),
            pltpu.VMEM((groups, 2, 2, planes, 2, rows, HEAD), BF16),
            pltpu.VMEM((groups, 2, rows, HEAD), BF16),
            pltpu.VMEM((total, 2 * rows), F32),
            pltpu.VMEM((total, 2 * rows), BF16),
            pltpu.VMEM((HEAD, total), BF16),
            pltpu.VMEM((HEAD, total), BF16),
            pltpu.VMEM((2, total, HEAD), F32),
            pltpu.SemaphoreType.DMA((groups, 2, ag_sems)),
            pltpu.SemaphoreType.DMA((groups, 2, ag_sems)),
            pltpu.SemaphoreType.DMA((groups, 2, rs_sems)),
            pltpu.SemaphoreType.DMA((groups, 2, rs_sems)),
        ],
        compiler_params=pltpu.CompilerParams(
            collective_id=0, has_side_effects=True, vmem_limit_bytes=58 * 1024 * 1024
        ),
        cost_estimate=pl.CostEstimate(
            flops=12 * queries.shape[0] * queries.shape[1] * total,
            bytes_accessed=8 * queries.size,
            transcendentals=queries.shape[0] * queries.shape[1] // HEAD * total,
        ),
    )(bias, queries, key_state_rows, value_state_rows, out_grad)


def solution(mesh):
    row = P(("dp", "ctx"), None)
    return jax.shard_map(
        body,
        mesh=mesh,
        in_specs=(P("dp"), P("dp"), row, row, row, row),
        out_specs=(row, row, row, row),
        check_vma=False,
    )
```

time: 444 us -> 147 us (0.33)
  waiting for transfers between devices: 211 us -> 0 us
  Pallas kernels: 0 us -> 137 us
  local copies, waits for them, and re-layouts: 101 us -> 6.47 us
  matrix products: 89.4 us -> 0 us
  between operations: 13.9 us -> 0.68 us
  other arithmetic: 15.7 us -> 2.9 us
  loops' own time: 10.4 us -> 0 us
    pallas_call x0 -> x1, Pallas kernels: none -> 137 us  [body(): pl.pallas_call(functools.partial(kernel, planes, groups, pairs), out_shap...]
    all_gather x2 -> x0, waiting for transfers between devices: 120 us -> none  [the longest x1 60.2 us: body(): lax.all_gather(value_state_rows, 'ctx', axis=0, tiled=True)]
    reduce_scatter x1 -> x0, waiting for transfers between devices: 89.8 us -> none  [body(): lax.psum_scatter(both_slots.astype(jnp.bfloat16), 'ctx', scatter_dimensio...]
    dot_general x28 -> x0, matrix products: 89.4 us -> none  [the longest x4 17.1 us: backward_step(): jnp.einsum('qgjd,kgd->gjqk', block_query, window_keys, preferred_element_...]
    slice x5 -> x0, local copies, waits for them, and re-layouts: 28.3 us -> none  [the longest x4 26.6 us: to_slots(): trimmed = buffer[span_rows:].reshape(blocks_all, BLK, head_width)]
    dynamic_slice x21 -> x0, local copies, waits for them, and re-layouts: 22.3 us -> none  [the longest x12 8.53 us: body(): lax.map(forward_block, (query_blocks, own_blocks))]
    reshape x20 -> x0, local copies, waits for them, and re-layouts: 14 us -> none  [the longest x2 6.86 us: to_slots(): trimmed = buffer[span_rows:].reshape(blocks_all, BLK, head_width)]
    gather x4 -> x0, local copies, waits for them, and re-layouts: 11.6 us -> none  [the longest x2 5.83 us: body(): blocked = gathered_rows.reshape(blocks_all, BLK, head_width)[slot_of]]
  transfers between devices with their start and end apart: 3 -> 0, of which waited for: 3 -> 0; matrix products, arithmetic and copies ran while one was open for 2% -> 0% of each run, Pallas kernels for 0% -> 0%
where the time goes in v1:
time: 147 us
  Pallas kernels  137 us (93%)
  local copies, waits for them, and re-layouts  6.47 us (4%)
  other arithmetic  2.9 us (2%)
    pallas_call x1, Pallas kernels, body(): pl.pallas_call(functools.partial(kernel, planes, groups, pairs), out_shap...  137 us
    unnamed x14, local copies, waits for them, and re-layouts  6.31 us

profile of v1, /device:TPU:0, one launch (start us, length us, event | category | flops | bytes accessed | tf_op | source)
XLA Modules:
  0.0 146.8 jit_solution(1680488515723328374)
XLA Ops:
  0.6 0.0 copy-start.4
  0.6 0.6 copy-done.4
  1.3 0.1 dynamic-slice_multiply_fusion
  1.4 0.0 copy-start.3
  1.4 0.7 copy-done.3
  2.0 0.2 reduce-window.8
  2.2 0.1 iota_add_fusion.1
  2.3 0.1 add.55
  2.4 0.1 convert_reduce_fusion.1
  2.4 0.1 iota_add_fusion
  2.5 0.1 add.50
  2.6 0.1 convert_reduce_fusion
  2.7 2.3 %and_select_fusion.bias_ref = f32[2048,128]{1,0:T(8,128)} fusion(s32[128]{0:T(128)S(1)} %add.55, s32[128]{0:T(128)S(1)} %convert_reduce_fusion.1, s32[2048]{0:T(1024)S(1)} %add.50, s32[2048]{0:T(1024)S(1)} %convert_reduce_fusion), kind=kLoop, calls=%fused_computation | loop fusion | flops 1048576 | bytes 1065984 | tf_op jit(solution)/shard_map/jit(_where)/select_n | solution.py:314
  5.0 136.8 %shard_map.93 = (bf16[128,4096]{1,0:T(8,128)(2,1)}, bf16[128,4096]{1,0:T(8,128)(2,1)}, bf16[128,512]{1,0:T(8,128)(2,1)}, bf16[128,512]{1,0:T(8,128)(2,1)}) custom-call(f32[2048,128]{1,0:T(8,128)} %and_select_fusion.bias_ref, bf16[128,4096]{1,0:T(8,128)(2,1)} %q_ref.1, bf16[128,512]{1,0:T(8,128)(2,1)} %k_ref.1, bf16[128,512]{1,0:T(8,128)(2,1)} %v_ref.1, ...), custom_call_target="tpu_custom_call" | custom-call | flops 12884901888 | bytes 4194304 | tf_op jit(solution)/shard_map/pallas_call | solution.py:319
  141.8 0.0 copy-start
  141.8 2.4 %copy.14 = bf16[128,4096]{1,0:T(8,128)(2,1)} copy(bf16[128,4096]{1,0:T(8,128)(2,1)} %get-tuple-element.8) | data formatting | bytes 2097152
  144.2 0.0 copy-done
  144.2 0.0 copy-start.2
  144.2 1.0 copy.15
  145.2 0.1 copy-done.2
  145.2 0.0 copy-start.1
  145.2 0.7 copy.16
  145.9 0.3 copy-done.1
  146.2 0.7 copy.17
  (1 shorter events, 0.0 us)
Async XLA Ops:
  0.6 0.7 copy-start.4
  1.4 0.7 copy-start.3
  141.8 2.4 %copy-start = (bf16[128,4096]{1,0:T(8,128)(2,1)S(1)}, bf16[128,4096]{1,0:T(8,128)(2,1)}, u32[]{:S(2)}) copy-start(bf16[128,4096]{1,0:T(8,128)(2,1)} %get-tuple-element.9) | copy-start | bytes 3145732
  144.2 1.0 copy-start.2
  145.2 1.0 copy-start.1

commit v2 on v1

--- a/solution.py
+++ b/solution.py
@@ -26,7 +26,7 @@
     planes, groups, pairs,
     bias_ref, q_ref, k_ref, v_ref, do_ref,
     out_ref, dq_ref, dk_ref, dv_ref,
-    kvb, part, half, zbuf, lastb, s_buf, e_buf, kt, vt, acc,
+    kvb, part, half, zbuf, lastb, s_buf, e_buf, kt, vt, acc, sums,
     ag_send, ag_recv, rs_send, rs_recv,
 ):
     rows = q_ref.shape[0]
@@ -122,61 +122,89 @@
                     def _():
                         ag_down(g, v, j, z + j).wait_send()
 
-    def rs_half(g, v):
-        src = part.at[g, 0, :, 1 - y] if v == 0 else part.at[g, 1, :, :, 1 - x]
-        return remote(src, half.at[g, v], rs_send.at[g, v, 0], rs_recv.at[g, v, 0],
+    def rs_half(g, v, t):
+        src = part.at[g, 0, t, 1 - y] if v == 0 else part.at[g, 1, t, :, 1 - x]
+        index = 2 * planes + 1 + t
+        return remote(src, half.at[g, v, t], rs_send.at[g, v, index], rs_recv.at[g, v, index],
                       peer_y if v == 0 else peer_x)
 
     def rs_flow(g, v, way, t):
-        index = 1 + way * planes + t
+        index = way * planes + t
         return remote(half.at[g, v, t], zbuf.at[g, v, way, t], rs_send.at[g, v, index],
                       rs_recv.at[g, v, index], me + 4 - 8 * way)
 
     def rs_last(g, v):
-        index = 1 + 2 * planes
+        index = 2 * planes
         src = half.at[g, 0, z, 1 - x] if v == 0 else half.at[g, 1, z, 1 - y]
         return remote(src, lastb.at[g, v], rs_send.at[g, v, index], rs_recv.at[g, v, index],
                       peer_x if v == 0 else peer_y)
 
+    def joined(g, v, t):
+        own = part[g, 0, t, y] if v == 0 else part[g, 1, t, :, x]
+        return half[g, v, t].astype(F32) + own.astype(F32)
+
     def rs_step(k, g):
+        if k == 0:
+            for i in range(planes):
+                for v in range(2):
+                    @pl.when(top - i > z)
+                    def _():
+                        rs_half(g, v, top - i).start()
+
+                    @pl.when(i < z)
+                    def _():
+                        rs_half(g, v, i).start()
+            for v in range(2):
+                rs_half(g, v, z).start()
+            return
         for v in range(2):
-            if k == 0:
-                rs_half(g, v).start()
-                continue
-            if k == 1:
-                rs_half(g, v).wait_recv()
-                own = part[g, 0, :, y] if v == 0 else part[g, 1, :, :, x]
-                half[g, v] = (half[g, v].astype(F32) + own.astype(F32)).astype(BF16)
-            if k <= planes:
+            if k < planes:
                 s = k - 1
                 for way in range(2):
                     place = z if way == 0 else top - z
                     dist = top - (s - place)
                     t = dist if way == 0 else top - dist
 
-                    @pl.when(jnp.logical_and(s >= place, dist >= place))
-                    def _():
+                    @pl.when(jnp.logical_and(s >= place, dist > place))
+                    def _():
+                        rs_half(g, v, t).wait_recv()
+
+                        @pl.when(place == 0)
+                        def _():
+                            half[g, v, t] = joined(g, v, t).astype(BF16)
+
                         @pl.when(place > 0)
                         def _():
                             rs_flow(g, v, way, t).wait_recv()
-                            half[g, v, t] = (
-                                half[g, v, t].astype(F32) + zbuf[g, v, way, t].astype(F32)
-                            ).astype(BF16)
-
-                        @pl.when(dist > place)
-                        def _():
-                            rs_flow(g, v, way, t).start()
-            if k == planes:
+                            half[g, v, t] = (joined(g, v, t) + zbuf[g, v, way, t].astype(F32)).astype(BF16)
+
+                        rs_flow(g, v, way, t).start()
+            elif k == planes:
+                rs_half(g, v, z).wait_recv()
+                sums[...] = joined(g, v, z)
+
+                @pl.when(z > 0)
+                def _():
+                    rs_flow(g, v, 0, z).wait_recv()
+                    sums[...] += zbuf[g, v, 0, z].astype(F32)
+
+                @pl.when(z < top)
+                def _():
+                    rs_flow(g, v, 1, z).wait_recv()
+                    sums[...] += zbuf[g, v, 1, z].astype(F32)
+
+                half[g, v, z] = sums[...].astype(BF16)
                 rs_last(g, v).start()
-            if k == planes + 1:
+            else:
                 rs_last(g, v).wait_recv()
                 own = half[g, 0, z, x] if v == 0 else half[g, 1, z, y]
                 total = (own.astype(F32) + lastb[g, v].astype(F32)).astype(BF16)
                 cols = pl.ds(pl.multiple_of(g * HEAD, HEAD), HEAD)
                 (dk_ref if v == 0 else dv_ref)[:, cols] = total
-                rs_half(g, v).wait_send()
                 rs_last(g, v).wait_send()
                 for t in range(planes):
+                    rs_half(g, v, t).wait_send()
+
                     @pl.when(t > z)
                     def _():
                         rs_flow(g, v, 0, t).wait_send()
@@ -204,27 +232,30 @@
         kvb[g, 1, z, y, x] = v_ref[:, g * HEAD:(g + 1) * HEAD]
     pl.semaphore_wait(barrier, 2 + (z < top).astype(jnp.int32) + (z > 0).astype(jnp.int32))
 
-    for g in range(groups):
-        ag_step(0, g)
-    for k in range(1, steps):
-        ag_step(k, 0)
+    def ag_slot(slot):
+        for g in reversed(range(groups)):
+            if slot == 2 * g:
+                ag_step(0, g)
+        for g in range(groups):
+            if 0 < slot - 2 * g < steps:
+                ag_step(slot - 2 * g, g)
+
+    for slot in range(steps):
+        ag_slot(slot)
 
     points = 2 * pairs
 
     def beside(place, g, p):
+        here = g * points + 2 * p + place
+        for i in range(2 * (groups - 1)):
+            if (1 + 2 * i) % 2 == place:
+                @pl.when(here == 1 + 2 * i)
+                def _():
+                    ag_slot(steps + i)
         for k in range(steps):
-            point = min(k, points - 1)
-            if point % 2 != place:
-                continue
-
-            @pl.when(p == point // 2)
-            def _():
-                if k > 0:
-                    @pl.when(g < groups - 1)
-                    def _():
-                        ag_step(k, g + 1)
-
-                @pl.when(g > 0)
+            point = min(k if k == 0 else k + 1, points - 1)
+            if point % 2 == place:
+                @pl.when(jnp.logical_and(p == point // 2, g > 0))
                 def _():
                     rs_step(k, g - 1)
 
@@ -314,7 +345,7 @@
     bias = jnp.where(allowed, 0.0, -1e30).astype(F32)
 
     ag_sems = 3 * planes - 1
-    rs_sems = 2 * planes + 2
+    rs_sems = 3 * planes + 1
     vmem = pl.BlockSpec(memory_space=pltpu.VMEM)
     return pl.pallas_call(
         functools.partial(kernel, planes, groups, pairs),
@@ -337,6 +368,7 @@
             pltpu.VMEM((HEAD, total), BF16),
             pltpu.VMEM((HEAD, total), BF16),
             pltpu.VMEM((2, total, HEAD), F32),
+            pltpu.VMEM((2, rows, HEAD), F32),
             pltpu.SemaphoreType.DMA((groups, 2, ag_sems)),
             pltpu.SemaphoreType.DMA((groups, 2, ag_sems)),
             pltpu.SemaphoreType.DMA((groups, 2, rs_sems)),

time: 147 us -> 136 us (0.925)
  Pallas kernels: 137 us -> 126 us
    pallas_call x1, Pallas kernels: 137 us -> 126 us  [body(): pl.pallas_call(functools.partial(kernel, planes, groups, pairs), out_shap...]
where the time goes in v2:
time: 136 us
  Pallas kernels  126 us (93%)
  local copies, waits for them, and re-layouts  6.47 us (5%)
  other arithmetic  2.9 us (2%)
    pallas_call x1, Pallas kernels, body(): pl.pallas_call(functools.partial(kernel, planes, groups, pairs), out_shap...  126 us
    unnamed x14, local copies, waits for them, and re-layouts  6.31 us

profile of v2, /device:TPU:0, one launch (start us, length us, event | category | flops | bytes accessed | tf_op | source)
XLA Modules:
  0.0 136.0 jit_solution(5118320448308985518)
XLA Ops:
  0.6 0.0 copy-start.4
  0.6 0.6 copy-done.4
  1.3 0.1 dynamic-slice_multiply_fusion
  1.4 0.0 copy-start.3
  1.4 0.7 copy-done.3
  2.0 0.2 reduce-window.8
  2.2 0.1 iota_add_fusion.1
  2.3 0.1 add.55
  2.4 0.1 convert_reduce_fusion.1
  2.4 0.1 iota_add_fusion
  2.5 0.1 add.50
  2.6 0.1 convert_reduce_fusion
  2.7 2.3 %and_select_fusion.bias_ref = f32[2048,128]{1,0:T(8,128)} fusion(s32[128]{0:T(128)S(1)} %add.55, s32[128]{0:T(128)S(1)} %convert_reduce_fusion.1, s32[2048]{0:T(1024)S(1)} %add.50, s32[2048]{0:T(1024)S(1)} %convert_reduce_fusion), kind=kLoop, calls=%fused_computation | loop fusion | flops 1048576 | bytes 1065984 | tf_op jit(solution)/shard_map/jit(_where)/select_n | solution.py:345
  5.0 126.0 %shard_map.93 = (bf16[128,4096]{1,0:T(8,128)(2,1)}, bf16[128,4096]{1,0:T(8,128)(2,1)}, bf16[128,512]{1,0:T(8,128)(2,1)}, bf16[128,512]{1,0:T(8,128)(2,1)}) custom-call(f32[2048,128]{1,0:T(8,128)} %and_select_fusion.bias_ref, bf16[128,4096]{1,0:T(8,128)(2,1)} %q_ref.1, bf16[128,512]{1,0:T(8,128)(2,1)} %k_ref.1, bf16[128,512]{1,0:T(8,128)(2,1)} %v_ref.1, ...), custom_call_target="tpu_custom_call" | custom-call | flops 12884901888 | bytes 4194304 | tf_op jit(solution)/shard_map/pallas_call | solution.py:350
  131.0 0.0 copy-start
  131.0 2.4 %copy.14 = bf16[128,4096]{1,0:T(8,128)(2,1)} copy(bf16[128,4096]{1,0:T(8,128)(2,1)} %get-tuple-element.8) | data formatting | bytes 2097152
  133.4 0.0 copy-done
  133.4 0.0 copy-start.2
  133.4 1.0 copy.15
  134.4 0.1 copy-done.2
  134.4 0.0 copy-start.1
  134.4 0.7 copy.16
  135.1 0.3 copy-done.1
  135.4 0.7 copy.17
  (1 shorter events, 0.0 us)
Async XLA Ops:
  0.6 0.7 copy-start.4
  1.4 0.7 copy-start.3
  131.0 2.4 %copy-start = (bf16[128,4096]{1,0:T(8,128)(2,1)S(1)}, bf16[128,4096]{1,0:T(8,128)(2,1)}, u32[]{:S(2)}) copy-start(bf16[128,4096]{1,0:T(8,128)(2,1)} %get-tuple-element.9) | copy-start | bytes 3145732
  133.4 1.0 copy-start.2
  134.4 1.0 copy-start.1

commit v3 on v2

--- a/solution.py
+++ b/solution.py
@@ -24,11 +24,17 @@
 
 def kernel(
     planes, groups, pairs,
-    bias_ref, q_ref, k_ref, v_ref, do_ref,
+    place_ref, doc_ref, own_ref, q_hbm, k_ref, v_ref, do_hbm,
     out_ref, dq_ref, dk_ref, dv_ref,
-    kvb, part, half, zbuf, lastb, s_buf, e_buf, kt, vt, acc, sums,
+    kvb, part, half, zbuf, lastb, s_buf, e_buf, kt, vt, acc, sums, bias_ref, q_ref, do_ref, load_sem,
     ag_send, ag_recv, rs_send, rs_recv,
 ):
+    loads = (
+        pltpu.make_async_copy(q_hbm, q_ref, load_sem.at[0]),
+        pltpu.make_async_copy(do_hbm, do_ref, load_sem.at[1]),
+    )
+    for load in loads:
+        load.start()
     rows = q_ref.shape[0]
     tile = 4 * rows
     scale = HEAD ** (-0.5)
@@ -72,7 +78,83 @@
         ref = kvb.at[g, 0, plane, 1 - y] if v == 0 else kvb.at[g, 1, plane, :, 1 - x]
         return ag_copy(g, v, 2 * planes - 1 + plane, ref, peer_y if v == 0 else peer_x)
 
+    def one_up(g, v, j, plane):
+        return ag_copy(g, v, 1 + j, kvb.at[g, v, plane, y, x], me + 4)
+
+    def one_down(g, v, j, plane):
+        return ag_copy(g, v, planes + j, kvb.at[g, v, plane, y, x], me - 4)
+
+    def one_side(g, v, plane):
+        return ag_copy(g, v, 3 * planes - 1 + plane, kvb.at[g, v, plane, y, x],
+                       peer_x if v == 0 else peer_y)
+
+    def one_side_in(g, v, plane):
+        ref = kvb.at[g, 0, plane, y, 1 - x] if v == 0 else kvb.at[g, 1, plane, 1 - y, x]
+        return ag_copy(g, v, 3 * planes - 1 + plane, ref, peer_x if v == 0 else peer_y)
+
+    def ag_step_z(k, g):
+        for v in range(2):
+            if k == 0:
+                @pl.when(z < top)
+                def _():
+                    one_up(g, v, 0, z).start()
+
+                @pl.when(z > 0)
+                def _():
+                    one_down(g, v, 0, z).start()
+
+                one_side(g, v, z).start()
+            elif k <= planes:
+                if k < planes:
+                    @pl.when(z >= k)
+                    def _():
+                        one_up(g, v, k - 1, z - k).wait_recv()
+                        if k < top:
+                            @pl.when(z < top)
+                            def _():
+                                one_up(g, v, k, z - k).start()
+                        one_side(g, v, z - k).start()
+
+                    @pl.when(z + k <= top)
+                    def _():
+                        one_down(g, v, k - 1, z + k).wait_recv()
+                        if k < top:
+                            @pl.when(z > 0)
+                            def _():
+                                one_down(g, v, k, z + k).start()
+                        one_side(g, v, z + k).start()
+                j = k - 1
+                if j == 0:
+                    one_side_in(g, v, z).wait_recv()
+                    ag_last(g, v, z).start()
+                else:
+                    @pl.when(z >= j)
+                    def _():
+                        one_side_in(g, v, z - j).wait_recv()
+                        ag_last(g, v, z - j).start()
+
+                    @pl.when(z + j <= top)
+                    def _():
+                        one_side_in(g, v, z + j).wait_recv()
+                        ag_last(g, v, z + j).start()
+            else:
+                for plane in range(planes):
+                    ag_last_in(g, v, plane).wait_recv()
+                    ag_last(g, v, plane).wait_send()
+                    one_side(g, v, plane).wait_send()
+                for j in range(top):
+                    @pl.when(jnp.logical_and(z < top, z >= j))
+                    def _():
+                        one_up(g, v, j, z - j).wait_send()
+
+                    @pl.when(jnp.logical_and(z > 0, z + j <= top))
+                    def _():
+                        one_down(g, v, j, z + j).wait_send()
+
     def ag_step(k, g):
+        if g % 2 == 1:
+            ag_step_z(k, g)
+            return
         for v in range(2):
             if k == 0:
                 ag_first(g, v).start()
@@ -240,8 +322,20 @@
             if 0 < slot - 2 * g < steps:
                 ag_step(slot - 2 * g, g)
 
-    for slot in range(steps):
+    ag_slot(0)
+    ag_slot(1)
+    own_place = own_ref[0:1, :]
+    own_doc = own_ref[1:2, :]
+    for c in range(bias_ref.shape[0] // HEAD):
+        span = slice(c * HEAD, (c + 1) * HEAD)
+        place_col = jnp.broadcast_to(place_ref[:, span], (HEAD, HEAD)).T
+        doc_col = jnp.broadcast_to(doc_ref[:, span], (HEAD, HEAD)).T
+        allowed = jnp.logical_and(doc_col == own_doc, place_col <= own_place)
+        bias_ref[span, :] = jnp.where(allowed, 0.0, -1e30)
+    for slot in range(2, steps):
         ag_slot(slot)
+    for load in loads:
+        load.wait()
 
     points = 2 * pairs
 
@@ -341,12 +435,14 @@
     query_place = (own[:, None] * BLK + offset[None, :]).reshape(-1)
     key_doc = jnp.sum((bounds[None, :] <= key_place[:, None]).astype(jnp.int32), axis=1)
     query_doc = jnp.sum((bounds[None, :] <= query_place[:, None]).astype(jnp.int32), axis=1)
-    allowed = (key_doc[:, None] == query_doc[None, :]) & (key_place[:, None] <= query_place[None, :])
-    bias = jnp.where(allowed, 0.0, -1e30).astype(F32)
-
-    ag_sems = 3 * planes - 1
+    places = key_place.astype(F32)[None, :]
+    docs = key_doc.astype(F32)[None, :]
+    mine = jnp.stack([query_place, query_doc]).astype(F32)
+
+    ag_sems = 4 * planes - 1
     rs_sems = 3 * planes + 1
     vmem = pl.BlockSpec(memory_space=pltpu.VMEM)
+    hbm = pl.BlockSpec(memory_space=pl.ANY)
     return pl.pallas_call(
         functools.partial(kernel, planes, groups, pairs),
         out_shape=(
@@ -355,7 +451,7 @@
             jax.ShapeDtypeStruct(key_state_rows.shape, BF16),
             jax.ShapeDtypeStruct(key_state_rows.shape, BF16),
         ),
-        in_specs=[vmem] * 5,
+        in_specs=[vmem, vmem, vmem, hbm, vmem, vmem, hbm],
         out_specs=(vmem,) * 4,
         scratch_shapes=[
             pltpu.VMEM((groups, 2, planes, 2, 2, rows, HEAD), BF16),
@@ -369,6 +465,10 @@
             pltpu.VMEM((HEAD, total), BF16),
             pltpu.VMEM((2, total, HEAD), F32),
             pltpu.VMEM((2, rows, HEAD), F32),
+            pltpu.VMEM((total, rows), F32),
+            pltpu.VMEM(queries.shape, BF16),
+            pltpu.VMEM(queries.shape, BF16),
+            pltpu.SemaphoreType.DMA((2,)),
             pltpu.SemaphoreType.DMA((groups, 2, ag_sems)),
             pltpu.SemaphoreType.DMA((groups, 2, ag_sems)),
             pltpu.SemaphoreType.DMA((groups, 2, rs_sems)),
@@ -382,7 +482,7 @@
             bytes_accessed=8 * queries.size,
             transcendentals=queries.shape[0] * queries.shape[1] // HEAD * total,
         ),
-    )(bias, queries, key_state_rows, value_state_rows, out_grad)
+    )(places, docs, mine, queries, key_state_rows, value_state_rows, out_grad)
 
 
 def solution(mesh):

time: 136 us -> 137 us (level)
  Pallas kernels: 126 us -> 128 us
    select_n x1 -> x0, other arithmetic: 2.32 us -> none  [body(): bias = jnp.where(allowed, 0.0, -1e+30).astype(F32)]
    pallas_call x1, Pallas kernels: 126 us -> 128 us  [body(): pl.pallas_call(functools.partial(kernel, planes, groups, pairs), out_shap...]
where the time goes in v3:
time: 137 us
  Pallas kernels  128 us (93%)
  local copies, waits for them, and re-layouts  7.23 us (5%)
  other arithmetic  1.76 us (1%)
    pallas_call x1, Pallas kernels, body(): pl.pallas_call(functools.partial(kernel, planes, groups, pairs), out_shap...  128 us
    unnamed x14, local copies, waits for them, and re-layouts  6.31 us

profile of v3, /device:TPU:0, one launch (start us, length us, event | category | flops | bytes accessed | tf_op | source)
XLA Modules:
  0.0 137.2 jit_solution(7922912523018883666)
XLA Ops:
  0.6 0.0 copy-start.4
  0.6 0.6 copy-done.4
  1.3 0.1 dynamic-slice_multiply_fusion
  1.4 0.0 copy-start.3
  1.4 0.7 copy-done.3
  2.0 0.2 reduce-window.8
  2.2 0.1 iota_add_fusion.1
  2.3 0.1 add.71
  2.4 0.1 add.70
  2.4 0.1 convert_reduce_fusion.1
  2.5 0.6 add_convert_fusion.own_ref
  3.1 0.1 iota_add_fusion
  3.2 0.1 add.65
  3.3 0.1 convert_reduce_fusion
  3.4 0.6 convert_element_type.38
  4.0 0.7 convert_element_type.36.place_ref
  4.6 127.5 %shard_map.93 = (bf16[128,4096]{1,0:T(8,128)(2,1)}, bf16[128,4096]{1,0:T(8,128)(2,1)}, bf16[128,512]{1,0:T(8,128)(2,1)}, bf16[128,512]{1,0:T(8,128)(2,1)}) custom-call(f32[1,2048]{1,0:T(1,128)} %convert_element_type.36.place_ref, f32[1,2048]{1,0:T(1,128)} %bitcast.4, f32[2,128]{1,0:T(2,128)} %add_convert_fusion.own_ref, bf16[128,4096]{1,0:T(8,128)(2,1)} %q_hbm.1, ...), custom_call_target="tpu_custom_call" | custom-call | flops 12884901888 | bytes 4194304 | tf_op jit(solution)/shard_map/pallas_call | solution.py:446
  132.2 0.0 copy-start
  132.2 2.4 %copy.14 = bf16[128,4096]{1,0:T(8,128)(2,1)} copy(bf16[128,4096]{1,0:T(8,128)(2,1)} %get-tuple-element.10) | data formatting | bytes 2097152
  134.6 0.0 copy-done
  134.6 0.0 copy-start.2
  134.6 1.0 copy.15
  135.5 0.1 copy-done.2
  135.6 0.0 copy-start.1
  135.6 0.7 copy.16
  136.3 0.3 copy-done.1
  136.5 0.7 copy.17
  (1 shorter events, 0.0 us)
Async XLA Ops:
  0.6 0.7 copy-start.4
  1.4 0.7 copy-start.3
  132.2 2.4 %copy-start = (bf16[128,4096]{1,0:T(8,128)(2,1)S(1)}, bf16[128,4096]{1,0:T(8,128)(2,1)}, u32[]{:S(2)}) copy-start(bf16[128,4096]{1,0:T(8,128)(2,1)} %get-tuple-element.11) | copy-start | bytes 3145732
  134.6 1.0 copy-start.2
  135.6 1.0 copy-start.1
